TPU v7x, 32 devices: a whole 2x2x4 slice. The times are simulated.
32 devices in a mesh: clip: 4 (over y, x), chan: 8 (over z, core).
Axes of the slice: x: 2, y: 2, z: 4, core: 2. Of those that a mesh axis runs over, the one named last changes fastest.
Arguments:
- features: bfloat16 [128, 196, 1024], P(('clip', 'chan')), may hold values from -6 to 6
- cotangent: bfloat16 [128, 196, 1024], P(('clip', 'chan')), may hold values from -6 to 6
- frame_counts: int32 [4], replicated, may hold values from 8 to 32, as said below
- weight_first: float32 [3, 1024, 256], P(None, 'chan'), may hold values from -0.109375 to 0.109375
- weight_middle: float32 [9, 256, 256], P(None, 'chan'), may hold values from -0.125 to 0.125
- weight_last: float32 [256, 1024], P('chan'), may hold values from -0.375 to 0.375
- weight_embed: float32 [1024, 3, 512], P('chan'), may hold values from -0.1875 to 0.1875
- weight_back: float32 [512, 1024], P('chan'), may hold values from -0.25 to 0.25
- norm_params: float32 [5120], replicated, may hold values from 0.5 to 1.5
- moment_first: float32 [3, 1024, 256], P(None, 'chan'), may hold values from -0.0008544922 to 0.0008544922
- moment_middle: float32 [9, 256, 256], P(None, 'chan'), may hold values from -0.0008544922 to 0.0008544922
- moment_last: float32 [256, 1024], P('chan'), may hold values from -0.0008544922 to 0.0008544922
- moment_embed: float32 [1024, 3, 512], P('chan'), may hold values from -0.0008544922 to 0.0008544922
- moment_back: float32 [512, 1024], P('chan'), may hold values from -0.0008544922 to 0.0008544922
- moment_norm: float32 [5120], replicated, may hold values from -0.0024414062 to 0.0024414062
- second_first: float32 [3, 1024, 256], P(None, 'chan'), may hold values from 2.6733165e-09 to 1.0693266e-08
- second_middle: float32 [9, 256, 256], P(None, 'chan'), may hold values from 2.6733165e-09 to 1.0693266e-08
- second_last: float32 [256, 1024], P('chan'), may hold values from 2.6733165e-09 to 1.0693266e-08
- second_embed: float32 [1024, 3, 512], P('chan'), may hold values from 2.6733165e-09 to 1.0693266e-08
- second_back: float32 [512, 1024], P('chan'), may hold values from 2.6733165e-09 to 1.0693266e-08
- second_norm: float32 [5120], replicated, may hold values from 1.33665825e-08 to 5.346633e-08
Outputs:
- mixed: bfloat16 [128, 196, 1024], P(('clip', 'chan'))
- features_gradient: bfloat16 [128, 196, 1024], P(('clip', 'chan'))
- first_gradient: float32 [3, 1024, 256], replicated
- middle_gradient: float32 [9, 256, 256], replicated
- last_gradient: float32 [256, 1024], replicated
- embed_gradient: float32 [1024, 3, 512], replicated
- back_gradient: float32 [512, 1024], replicated
- norm_gradient: float32 [5120], replicated
- moment_first_new: float32 [3, 1024, 256], P(None, 'chan')
- moment_middle_new: float32 [9, 256, 256], P(None, 'chan')
- moment_last_new: float32 [256, 1024], P('chan')
- moment_embed_new: float32 [1024, 3, 512], P('chan')
- moment_back_new: float32 [512, 1024], P('chan')
- moment_norm_new: float32 [5120], replicated
- second_first_new: float32 [3, 1024, 256], P(None, 'chan')
- second_middle_new: float32 [9, 256, 256], P(None, 'chan')
- second_last_new: float32 [256, 1024], P('chan')
- second_embed_new: float32 [1024, 3, 512], P('chan')
- second_back_new: float32 [512, 1024], P('chan')
- second_norm_new: float32 [5120], replicated
- weight_first_new: float32 [3, 1024, 256], P(None, 'chan')
- weight_middle_new: float32 [9, 256, 256], P(None, 'chan')
- weight_last_new: float32 [256, 1024], P('chan')
- weight_embed_new: float32 [1024, 3, 512], P('chan')
- weight_back_new: float32 [512, 1024], P('chan')
- norm_params_new: float32 [5120], replicated
- gradient_norm: float32 [], replicated
Inputs may be any that keep to these rules, and one draw needn't show every extreme that they name: `frame_counts`: each clip has 8, 16 or 32 valid frames, and some clip has 32.
All inputs are finite; a program needn't handle non-finite values.
Results may differ from a plain program's by a relative error of at most 0.035.
Values may be sent and summed in bfloat16 or wider, within the bound.
No kernel may reach another device: no remote copies, remote signals or barrier semaphores. Data moves between devices by JAX's collectives and lax.ppermute only.
A program may use at most 256 MiB of HBM per device.

v0:
```python
import jax
import jax.numpy as jnp
from jax import lax
from jax.sharding import PartitionSpec as P

D = 1024
BOT = 256
INNER = 512
HH = 14
WW = 14
STEP = 10
DPC = 8


EPS_NORM = 1e-05
BETA_ONE = 0.9
BETA_TWO = 0.95
ADAM_EPS = 1e-08
WEIGHT_DECAY = 0.01
CLIP_AT = 1.0
GAIN_RATE = 0.5
MASKED = -1e30


def swapped(value, axis, apart):
    mask = 2**apart
    pairs = [(source, source ^ mask) for source in range(lax.axis_size(axis))]
    return lax.ppermute(value, axis, pairs)


def with_halo(cells, sides, width):
    for axis, dim in sides:
        count = lax.axis_size(axis)
        ends = count - 1
        head = lax.slice_in_dim(cells, 0, width, axis=dim)
        tail = lax.slice_in_dim(cells, cells.shape[dim] - width, cells.shape[dim], axis=dim)
        cells = jnp.concatenate(
            [
                lax.ppermute(tail, axis, [(i, (i + 1) % count) for i in range(ends)]),
                cells,
                lax.ppermute(head, axis, [((i + 1) % count, i) for i in range(ends)]),
            ],
            axis=dim,
        )
    return cells


def batch_stats(values, valid_rows, row_total):
    sums = lax.psum(
        (jnp.sum(values * valid_rows, axis=0), jnp.sum(values * values * valid_rows, axis=0)),
        ("clip", "chan"),
    )
    mean = sums[0] / row_total
    scales = lax.rsqrt(sums[1] / row_total - mean * mean + EPS_NORM)
    return ((values - mean) * scales, scales)


def batch_back(incoming, normal, scales, gains, valid_rows, row_total):
    sums = lax.psum(
        (jnp.sum(incoming, axis=0), jnp.sum(incoming * normal, axis=0)), ("clip", "chan")
    )
    removed = (sums[0] + normal * sums[1]) / row_total
    return (valid_rows * gains * scales * (incoming - removed), sums[1], sums[0])


def silu_slope(values):
    sigmoid = jax.nn.sigmoid(values)
    return sigmoid * (1.0 + values * (1.0 - sigmoid))


def trim_rims(padded, clip_place):
    left_ok = (clip_place > 0).astype(padded.dtype)
    right_ok = (clip_place < DPC - 1).astype(padded.dtype)
    return jnp.concatenate([padded[:1] * left_ok, padded[1:-1], padded[-1:] * right_ok], axis=0)


def spatial_cols(values, frames):
    channels = values.shape[-1]
    grid = values.reshape(frames, HH, WW, channels)
    padded = jnp.pad(grid, ((0, 0), (1, 1), (1, 1), (0, 0)))
    tap_list = [
        padded[:, row_tap : row_tap + HH, col_tap : col_tap + WW]
        for row_tap in range(3)
        for col_tap in range(3)
    ]
    return jnp.concatenate(tap_list, axis=-1).reshape(frames * HH * WW, 9 * channels)


def spatial_back(columns, frames):
    channels = columns.shape[-1] // 9
    grid = columns.reshape(frames, HH, WW, 9, channels)
    padded = jnp.zeros((frames, HH + 2, WW + 2, channels), jnp.float32)
    for row_tap in range(3):
        for col_tap in range(3):
            padded = padded.at[:, row_tap : row_tap + HH, col_tap : col_tap + WW].add(
                grid[:, :, :, 3 * row_tap + col_tap]
            )
    return padded[:, 1:-1, 1:-1].reshape(frames * HH * WW, channels)


def gather_clip(pairs, chan_at):
    current = pairs
    for level in range(DPC.bit_length() - 1):
        partner = swapped(current, "chan", level)
        lower = chan_at >> level & 1 == 0
        current = jnp.where(
            lower,
            jnp.concatenate([current, partner], axis=0),
            jnp.concatenate([partner, current], axis=0),
        )
    return current


def sum_clip(pairs, chan_at):
    current = pairs
    for level in reversed(range(DPC.bit_length() - 1)):
        half_rows = current.shape[0] // 2
        lower = chan_at >> level & 1 == 0
        kept = jnp.where(lower, current[:half_rows], current[half_rows:])
        outgoing = jnp.where(lower, current[half_rows:], current[:half_rows])
        current = kept + swapped(outgoing.astype(jnp.bfloat16), "chan", level).astype(
            outgoing.dtype
        )
    return current


def adam_step(master, gradient, moment, second, factor, rate):
    clipped = gradient * factor
    moment_new = BETA_ONE * moment + (1.0 - BETA_ONE) * clipped
    second_new = BETA_TWO * second + (1.0 - BETA_TWO) * clipped * clipped
    moment_hat = moment_new / (1.0 - BETA_ONE**STEP)
    second_hat = second_new / (1.0 - BETA_TWO**STEP)
    master_new = master - rate * (
        moment_hat / (jnp.sqrt(second_hat) + ADAM_EPS) + WEIGHT_DECAY * master
    )
    return (moment_new, second_new, master_new)


def body(
    features,
    cotangent,
    frame_counts,
    weight_first,
    weight_middle,
    weight_last,
    weight_embed,
    weight_back,
    norm_params,
    moment_first,
    moment_middle,
    moment_last,
    moment_embed,
    moment_back,
    moment_norm,
    second_first,
    second_middle,
    second_last,
    second_embed,
    second_back,
    second_norm,
):
    chan_at = lax.axis_index("chan")
    device = lax.axis_index("clip") * lax.axis_size("chan") + chan_at
    frames, spot_count, model_width = features.shape
    row_count = frames * spot_count
    narrow = BOT
    inner_width = INNER
    clip_place = chan_at % DPC
    clip_at = device // DPC
    clip_ids = jnp.arange(frame_counts.shape[0], dtype=jnp.int32)
    length = jnp.sum(jnp.where(clip_ids == clip_at, frame_counts, 0))
    local_frames = clip_place * frames + jnp.arange(frames, dtype=jnp.int32)
    frame_ok = (local_frames < length).astype(jnp.float32)
    valid_rows = jnp.repeat(frame_ok, spot_count)[:, None]
    row_total = jnp.sum(frame_counts).astype(jnp.float32) * spot_count
    key_ok = jnp.repeat(
        (jnp.arange(DPC * frames, dtype=jnp.int32) < length).astype(jnp.float32), spot_count
    )
    span_list = [narrow] * 4 + [model_width] * 4
    starts = [sum(span_list[:index]) for index in range(8)]
    pieces = [norm_params[starts[index] : starts[index] + span_list[index]] for index in range(8)]
    gain_one, shift_one, gain_two, shift_two, gain_three, shift_three, gain_four, shift_four = (
        pieces
    )
    first_low, middle_low, last_low, embed_low, back_low = (
        lax.all_gather(weight_first.astype(jnp.bfloat16), "chan", axis=1, tiled=True),
        lax.all_gather(weight_middle.astype(jnp.bfloat16), "chan", axis=1, tiled=True),
        lax.all_gather(weight_last.astype(jnp.bfloat16), "chan", axis=0, tiled=True),
        lax.all_gather(weight_embed.astype(jnp.bfloat16), "chan", axis=0, tiled=True),
        lax.all_gather(weight_back.astype(jnp.bfloat16), "chan", axis=0, tiled=True),
    )
    masked = features * frame_ok.astype(jnp.bfloat16)[:, None, None]
    padded = trim_rims(with_halo(masked, (("chan", 0),), 1), clip_place)
    first_cols = jnp.concatenate(
        [padded[offset : offset + frames] for offset in range(3)], axis=-1
    ).reshape(row_count, 3 * model_width)
    first_pre = jnp.dot(
        first_cols, first_low.reshape(3 * model_width, narrow), preferred_element_type=jnp.float32
    )
    normal_one, scale_one = batch_stats(first_pre, valid_rows, row_total)
    act_one_pre = normal_one * gain_one + shift_one
    act_one = (jax.nn.silu(act_one_pre) * valid_rows).astype(jnp.bfloat16)
    middle_cols = spatial_cols(act_one, frames)
    middle_pre = jnp.dot(
        middle_cols, middle_low.reshape(9 * narrow, narrow), preferred_element_type=jnp.float32
    )
    normal_two, scale_two = batch_stats(middle_pre, valid_rows, row_total)
    act_two_pre = normal_two * gain_two + shift_two
    act_two = (jax.nn.silu(act_two_pre) * valid_rows).astype(jnp.bfloat16)
    last_pre = jnp.dot(act_two, last_low, preferred_element_type=jnp.float32)
    normal_three, scale_three = batch_stats(last_pre, valid_rows, row_total)
    residual_pre = features.reshape(row_count, model_width).astype(jnp.float32) + (
        normal_three * gain_three + shift_three
    )
    residual_out = jax.nn.silu(residual_pre) * valid_rows
    residual_low = residual_out.astype(jnp.bfloat16)
    projected = jnp.dot(
        residual_low,
        embed_low.reshape(model_width, 3 * inner_width),
        preferred_element_type=jnp.float32,
    ).astype(jnp.bfloat16)
    query = projected[:, :inner_width]
    clip_pairs = gather_clip(projected[:, inner_width:], chan_at)
    keys_all = clip_pairs[:, :inner_width]
    values_all = clip_pairs[:, inner_width:]
    scaling = inner_width ** (-0.5)
    scores = jnp.einsum("qd,kd->qk", query, keys_all, preferred_element_type=jnp.float32) * scaling
    scores = jnp.where(key_ok[None, :] > 0, scores, MASKED)
    row_peak = jnp.max(scores, axis=1, keepdims=True)
    lifted = jnp.exp(scores - row_peak) * key_ok[None, :]
    row_sums = jnp.sum(lifted, axis=1, keepdims=True)
    weights = lifted / row_sums
    log_total = row_peak + jnp.log(row_sums)
    attended = jnp.dot(
        weights.astype(jnp.bfloat16), values_all, preferred_element_type=jnp.float32
    ).astype(jnp.bfloat16)
    attn_pre = jnp.dot(attended, back_low, preferred_element_type=jnp.float32)
    normal_four, scale_four = batch_stats(attn_pre, valid_rows, row_total)
    mixed = (
        ((residual_out + (normal_four * gain_four + shift_four)) * valid_rows)
        .astype(jnp.bfloat16)
        .reshape(frames, spot_count, model_width)
    )
    outer_grad = cotangent.reshape(row_count, model_width).astype(jnp.float32) * valid_rows
    attn_grad, gain_four_grad, shift_four_grad = batch_back(
        outer_grad, normal_four, scale_four, gain_four, valid_rows, row_total
    )
    attn_grad = attn_grad.astype(jnp.bfloat16)
    back_local = jnp.einsum("rd,re->de", attended, attn_grad, preferred_element_type=jnp.float32)
    attended_grad = jnp.einsum(
        "re,de->rd", attn_grad, back_low, preferred_element_type=jnp.float32
    ).astype(jnp.bfloat16)
    again = jnp.einsum("qd,kd->qk", query, keys_all, preferred_element_type=jnp.float32) * scaling
    again = jnp.where(key_ok[None, :] > 0, again, MASKED)
    weights = jnp.exp(again - log_total) * key_ok[None, :]
    prob_grad = jnp.einsum(
        "qd,kd->qk", attended_grad, values_all, preferred_element_type=jnp.float32
    )
    row_term = jnp.sum(weights * prob_grad, axis=1, keepdims=True)
    score_grad = (weights * (prob_grad - row_term)).astype(jnp.bfloat16)
    query_grad = (
        jnp.dot(score_grad, keys_all, preferred_element_type=jnp.float32) * scaling
    ).astype(jnp.bfloat16)
    key_grad = (
        jnp.einsum("qk,qd->kd", score_grad, query, preferred_element_type=jnp.float32) * scaling
    )
    value_grad = jnp.einsum(
        "qk,qd->kd", weights.astype(jnp.bfloat16), attended_grad, preferred_element_type=jnp.float32
    )
    pair_grad = sum_clip(jnp.concatenate([key_grad, value_grad], axis=1), chan_at).astype(
        jnp.bfloat16
    )
    projected_grad = jnp.concatenate([query_grad, pair_grad], axis=1)
    embed_local = jnp.einsum(
        "rd,re->de", residual_low, projected_grad, preferred_element_type=jnp.float32
    ).reshape(model_width, 3, inner_width)
    residual_grad = outer_grad + jnp.einsum(
        "re,de->rd",
        projected_grad,
        embed_low.reshape(model_width, 3 * inner_width),
        preferred_element_type=jnp.float32,
    )
    pre_grad = residual_grad * valid_rows * silu_slope(residual_pre)
    last_grad, gain_three_grad, shift_three_grad = batch_back(
        pre_grad, normal_three, scale_three, gain_three, valid_rows, row_total
    )
    last_grad = last_grad.astype(jnp.bfloat16)
    last_local = jnp.einsum("rc,rd->cd", act_two, last_grad, preferred_element_type=jnp.float32)
    two_grad = (
        jnp.einsum("rd,cd->rc", last_grad, last_low, preferred_element_type=jnp.float32)
        * valid_rows
        * silu_slope(act_two_pre)
    )
    middle_grad, gain_two_grad, shift_two_grad = batch_back(
        two_grad, normal_two, scale_two, gain_two, valid_rows, row_total
    )
    middle_grad = middle_grad.astype(jnp.bfloat16)
    middle_local = jnp.einsum(
        "rk,rc->kc", middle_cols, middle_grad, preferred_element_type=jnp.float32
    ).reshape(9, narrow, narrow)
    column_grad = jnp.einsum(
        "rc,kc->rk",
        middle_grad,
        middle_low.reshape(9 * narrow, narrow),
        preferred_element_type=jnp.float32,
    )
    one_grad = spatial_back(column_grad, frames) * valid_rows * silu_slope(act_one_pre)
    first_grad, gain_one_grad, shift_one_grad = batch_back(
        one_grad, normal_one, scale_one, gain_one, valid_rows, row_total
    )
    first_grad = first_grad.astype(jnp.bfloat16)
    first_local = jnp.einsum(
        "rk,rc->kc", first_cols, first_grad, preferred_element_type=jnp.float32
    ).reshape(3, model_width, narrow)
    grad_padded = trim_rims(
        with_halo(first_grad.reshape(frames, spot_count, narrow), (("chan", 0),), 1), clip_place
    )
    back_cols = jnp.stack(
        [grad_padded[2 - offset : 2 - offset + frames] for offset in range(3)], axis=2
    ).reshape(row_count, 3, narrow)
    conv_back = jnp.einsum("rtc,tdc->rd", back_cols, first_low, preferred_element_type=jnp.float32)
    features_gradient = (
        (conv_back * valid_rows + pre_grad)
        .astype(jnp.bfloat16)
        .reshape(frames, spot_count, model_width)
    )
    local_terms = (first_local, middle_local, last_local, embed_local, back_local)
    summed = lax.psum(
        (local_terms[0], local_terms[1], local_terms[2], local_terms[3], local_terms[4]),
        ("clip", "chan"),
    )
    norm_gradient = jnp.concatenate(
        [
            gain_one_grad,
            shift_one_grad,
            gain_two_grad,
            shift_two_grad,
            gain_three_grad,
            shift_three_grad,
            gain_four_grad,
            shift_four_grad,
        ]
    )
    all_grads = tuple(summed) + (norm_gradient,)
    gradient_norm = jnp.sqrt(sum((jnp.sum(item * item) for item in all_grads)))
    factor = jnp.minimum(1.0, CLIP_AT / (gradient_norm + 1e-06))
    masters = (weight_first, weight_middle, weight_last, weight_embed, weight_back)
    moments = (moment_first, moment_middle, moment_last, moment_embed, moment_back)
    seconds = (second_first, second_middle, second_last, second_embed, second_back)
    shard_axes = (1, 1, 0, 0, 0)
    fans = (3 * D, 9 * BOT, BOT, D, INNER)
    results = []
    for index in range(5):
        span = masters[index].shape[shard_axes[index]]
        owned = lax.dynamic_slice_in_dim(all_grads[index], chan_at * span, span, shard_axes[index])
        results.append(
            adam_step(
                masters[index],
                owned,
                moments[index],
                seconds[index],
                factor,
                0.5 * fans[index] ** (-0.5),
            )
        )
    results.append(
        adam_step(norm_params, norm_gradient, moment_norm, second_norm, factor, GAIN_RATE)
    )
    return (
        mixed,
        features_gradient,
        all_grads[0],
        all_grads[1],
        all_grads[2],
        all_grads[3],
        all_grads[4],
        all_grads[5],
        results[0][0],
        results[1][0],
        results[2][0],
        results[3][0],
        results[4][0],
        results[5][0],
        results[0][1],
        results[1][1],
        results[2][1],
        results[3][1],
        results[4][1],
        results[5][1],
        results[0][2],
        results[1][2],
        results[2][2],
        results[3][2],
        results[4][2],
        results[5][2],
        gradient_norm,
    )


def solution(mesh):
    placed = (
        P(("clip", "chan"), None, None),
        P(("clip", "chan"), None, None),
        P(),
        P(None, "chan", None),
        P(None, "chan", None),
        P("chan", None),
        P("chan", None, None),
        P("chan", None),
        P(),
        P(None, "chan", None),
        P(None, "chan", None),
        P("chan", None),
        P("chan", None, None),
        P("chan", None),
        P(),
        P(None, "chan", None),
        P(None, "chan", None),
        P("chan", None),
        P("chan", None, None),
        P("chan", None),
        P(),
    )
    return jax.shard_map(
        body,
        mesh=mesh,
        in_specs=placed,
        out_specs=(
            P(("clip", "chan"), None, None),
            P(("clip", "chan"), None, None),
            P(),
            P(),
            P(),
            P(),
            P(),
            P(),
            P(None, "chan", None),
            P(None, "chan", None),
            P("chan", None),
            P("chan", None, None),
            P("chan", None),
            P(),
            P(None, "chan", None),
            P(None, "chan", None),
            P("chan", None),
            P("chan", None, None),
            P("chan", None),
            P(),
            P(None, "chan", None),
            P(None, "chan", None),
            P("chan", None),
            P("chan", None, None),
            P("chan", None),
            P(),
            P(),
        ),
        check_vma=False,
    )
```

profile of v0, /device:TPU:0, one launch (start us, length us, event | category | flops | bytes accessed | tf_op | source)
XLA Modules:
  0.0 1720.9 jit_solution(1635596724462427495)
XLA Ops:
  18.6 3.8 collective-permute-start
  23.6 26.9 %all_gather.17 = bf16[256,1024]{1,0:T(8,128)(2,1)} all-gather(bf16[32,1024]{1,0:T(8,128)(2,1)S(1)} %convert_element_type.140), channel_id=1, replica_groups=mesh['clip'=4,'chan'=8] {'chan'}, dimensions={0}, use_global_device_ids=true | all-gather | bytes 589824 | tf_op jit(solution)/shard_map/all_gather | solution.py:188
  58.6 5.7 fusion.13
  64.3 4.4 reshape.553
  68.7 4.3 multiply_reduce_fusion.17
  73.0 43.2 %all-reduce.9 = (f32[256]{0:T(256)S(1)}, f32[256]{0:T(256)S(1)}) all-reduce(f32[256]{0:T(256)S(1)} %get-tuple-element.252, f32[256]{0:T(256)S(1)} %get-tuple-element.251), channel_id=1, replica_groups=mesh['clip'=4,'chan'=8] {'clip','chan'}, use_global_device_ids=true, to_apply=%region_2.3 | all-reduce | flops 512 | bytes 4096 | tf_op jit(solution)/shard_map/psum | solution.py:49
  117.7 4.6 pad_slice_fusion.2
  137.8 4.4 multiply_reduce_fusion.15
  142.2 41.1 %all-reduce.8 = (f32[256]{0:T(256)S(1)}, f32[256]{0:T(256)S(1)}) all-reduce(f32[256]{0:T(256)S(1)} %get-tuple-element.250, f32[256]{0:T(256)S(1)} %get-tuple-element.249), channel_id=1, replica_groups=mesh['clip'=4,'chan'=8] {'clip','chan'}, use_global_device_ids=true, to_apply=%region_7.8 | all-reduce | flops 512 | bytes 4096 | tf_op jit(solution)/shard_map/psum | solution.py:49
  183.4 4.0 multiply_reduce_fusion.8
  187.4 39.4 %all-reduce.7 = (f32[1024]{0:T(1024)S(1)}, f32[1024]{0:T(1024)S(1)}) all-reduce(f32[1024]{0:T(1024)S(1)} %get-tuple-element.246, f32[1024]{0:T(1024)S(1)} %get-tuple-element.245), channel_id=1, replica_groups=mesh['clip'=4,'chan'=8] {'clip','chan'}, use_global_device_ids=true, to_apply=%region_13.14 | all-reduce | flops 2048 | bytes 16384 | tf_op jit(solution)/shard_map/psum | solution.py:49
  226.8 4.8 multiply_multiply_fusion.1
  231.6 5.5 convolution_convert_fusion
  240.0 2.5 collective-permute-done.2
  242.5 3.4 maximum_select_fusion.2
  248.0 69.9 %collective-permute-done.3 = bf16[1568,1024]{1,0:T(8,128)(2,1)} collective-permute-done((bf16[1568,1024]{1,0:T(8,128)(2,1)S(1)}, bf16[1568,1024]{1,0:T(8,128)(2,1)}, u32[]{:S(2)}, u32[]{:S(2)}) %collective-permute-start.3) | collective-permute-done | bytes 3211296 | tf_op jit(solution)/shard_map/ppermute | solution.py:28
  317.9 7.2 maximum_select_fusion.1
  325.1 2.5 collective-permute-start.4
  329.7 3.7 copy.128
  338.0 274.3 %collective-permute-done.4 = bf16[3136,1024]{1,0:T(8,128)(2,1)} collective-permute-done((bf16[3136,1024]{1,0:T(8,128)(2,1)}, bf16[3136,1024]{1,0:T(8,128)(2,1)}, u32[]{:S(2)}, u32[]{:S(2)}) %collective-permute-start.4) | collective-permute-done | bytes 6422560 | tf_op jit(solution)/shard_map/ppermute | solution.py:28
  612.3 12.1 maximum_select_fusion
  624.4 12.3 fusion.2
  636.7 11.9 fusion
  648.6 12.6 fusion.24
  661.2 4.3 multiply_reduce_fusion.6
  665.5 38.4 %all-reduce.6 = (f32[1024]{0:T(1024)S(1)}, f32[1024]{0:T(1024)S(1)}) all-reduce(f32[1024]{0:T(1024)S(1)} %get-tuple-element.244, f32[1024]{0:T(1024)S(1)} %get-tuple-element.243), channel_id=1, replica_groups=mesh['clip'=4,'chan'=8] {'clip','chan'}, use_global_device_ids=true, to_apply=%region_19.20 | all-reduce | flops 2048 | bytes 16384 | tf_op jit(solution)/shard_map/psum | solution.py:49
  703.9 2.5 multiply_reduce_fusion.3
  706.5 41.7 %all-reduce.5 = (f32[1024]{0:T(1024)S(1)}, f32[1024]{0:T(1024)S(1)}) all-reduce(f32[1024]{0:T(1024)S(1)} %multiply_reduce_fusion.3, f32[1024]{0:T(1024)S(1)} %multiply_reduce_fusion.4), channel_id=1, replica_groups=mesh['clip'=4,'chan'=8] {'clip','chan'}, use_global_device_ids=true, to_apply=%region_23.24 | all-reduce | flops 2048 | bytes 16384 | tf_op jit(solution)/shard_map/psum | solution.py:59
  748.2 4.9 multiply_convert_fusion.2
  756.2 15.9 multiply_reduce_fusion
  772.1 13.3 fusion.3
  785.4 18.6 %multiply_convert_fusion = bf16[784,6272]{1,0:T(8,128)(2,1)S(1)} fusion(f32[784,6272]{1,0:T(8,128)} %get-tuple-element.344, f32[784]{0:T(1024)S(1)} %get-tuple-element.343, f32[6272]{0:T(1024)S(1)} %broadcast_in_dim_reshape.2, f32[784]{0:T(1024)S(1)} %log_add_fusion, f32[784,6272]{1,0:T(8,128)} %get-tuple-element.341, ...), kind=kLoop, calls=%fused_computation.2 | loop fusion | flops 34420736 | bytes 49210112 | tf_op jit(solution)/shard_map/convert_element_type | solution.py:260
  804.1 3.7 copy-done.13
  807.8 11.5 convolution_multiply_fusion
  819.3 9.0 select_convert_fusion
  828.9 277.0 %collective-permute-done.5 = bf16[3136,1024]{1,0:T(8,128)(2,1)} collective-permute-done((bf16[3136,1024]{1,0:T(8,128)(2,1)}, bf16[3136,1024]{1,0:T(8,128)(2,1)}, u32[]{:S(2)}, u32[]{:S(2)}) %collective-permute-start.5) | collective-permute-done | bytes 6422560 | tf_op jit(solution)/shard_map/ppermute | solution.py:28
  1105.9 11.7 convert_add_fusion
  1117.7 4.6 copy-done
  1126.4 7.5 copy.139
  1133.9 6.2 copy.141
  1140.2 4.3 fusion.81
  1144.4 51.8 %collective-permute-done.6 = bf16[1568,1024]{1,0:T(8,128)(2,1)} collective-permute-done((bf16[1568,1024]{1,0:T(8,128)(2,1)}, bf16[1568,1024]{1,0:T(8,128)(2,1)}, u32[]{:S(2)}, u32[]{:S(2)}) %collective-permute-start.6) | collective-permute-done | bytes 3211296 | tf_op jit(solution)/shard_map/ppermute | solution.py:28
  1196.3 7.4 convert_add_fusion.1
  1204.1 10.1 fusion.21
  1216.1 5.5 fusion.20
  1221.6 5.9 fusion.65
  1227.6 38.9 %all-reduce.4 = (f32[1024]{0:T(1024)S(1)}, f32[1024]{0:T(1024)S(1)}) all-reduce(f32[1024]{0:T(1024)S(1)} %get-tuple-element.248, f32[1024]{0:T(1024)S(1)} %get-tuple-element.247), channel_id=1, replica_groups=mesh['clip'=4,'chan'=8] {'clip','chan'}, use_global_device_ids=true, to_apply=%region_28.29 | all-reduce | flops 2048 | bytes 16384 | tf_op jit(solution)/shard_map/psum | solution.py:59
  1266.5 4.0 multiply_convert_fusion.1
  1273.3 40.5 %all-reduce.3 = (f32[256]{0:T(256)S(1)}, f32[256]{0:T(256)S(1)}) all-reduce(f32[256]{0:T(256)S(1)} %get-tuple-element.256, f32[256]{0:T(256)S(1)} %get-tuple-element.255), channel_id=1, replica_groups=mesh['clip'=4,'chan'=8] {'clip','chan'}, use_global_device_ids=true, to_apply=%region_32.33 | all-reduce | flops 512 | bytes 4096 | tf_op jit(solution)/shard_map/psum | solution.py:59
  1314.2 5.1 fusion.48
  1320.7 3.0 copy-done.2
  1325.3 3.0 scatter-add.31
  1328.3 3.3 add_select_fusion
  1331.6 3.0 scatter-add.34
  1356.0 40.0 %all-reduce.2 = (f32[256]{0:T(256)S(1)}, f32[256]{0:T(256)S(1)}) all-reduce(f32[256]{0:T(256)S(1)} %get-tuple-element.254, f32[256]{0:T(256)S(1)} %get-tuple-element.253), channel_id=1, replica_groups=mesh['clip'=4,'chan'=8] {'clip','chan'}, use_global_device_ids=true, to_apply=%region_37.38 | all-reduce | flops 512 | bytes 4096 | tf_op jit(solution)/shard_map/psum | solution.py:59
  1396.3 6.2 fusion.50
  1406.3 2.4 copy.148
  1412.2 3.1 collective-permute-done.8
  1415.5 5.1 fusion.16
  1424.9 239.1 %all-reduce.13.cloned.1.call-done = (f32[3,1024,256]{2,1,0:T(8,128)}, f32[9,256,256]{2,1,0:T(8,128)}, f32[256,1024]{1,0:T(8,128)}, f32[1024,3,512]{0,2,1:T(8,128)}, f32[512,1024]{1,0:T(8,128)}) async-done(((f32[3,1024,256]{2,1,0:T(8,128)}, f32[9,256,256]{2,1,0:T(8,128)}, f32[256,1024]{1,0:T(8,128)}, f32[1024,3,512]{0,2,1:T(8,128)}, f32[512,1024]{1,0:T(8,128)}), (f32[3,1024,256]{2,1,0:T(8,128)}, ...) | async-done | bytes 14942224 | tf_op jit(solution)/shard_map/psum | solution.py:328
  1664.0 5.0 multiply_reduce_fusion.1
  1669.0 6.7 copy.150
  1675.8 3.0 multiply_reduce_fusion.10
  1686.2 3.6 multiply_subtract_fusion
  (304 shorter events, 124.0 us)
Async XLA Ops:
  7.2 15.2 copy-start.30
  7.2 61.5 %all-gather.5.cloned.1.call-start = ((), (), s32[]{:S(2)}) async-start(), calls=%async_computation | async-start | bytes 1769472 | tf_op jit(solution)/shard_map/all_gather | solution.py:186
  9.0 128.8 %all-gather.7.cloned.1.call-start = ((), (), s32[]{:S(2)}) async-start(), calls=%async_computation.1 | async-start | bytes 1327104 | tf_op jit(solution)/shard_map/all_gather | solution.py:187
  10.8 220.9 %all-gather.9.cloned.1.call-start = ((), (), s32[]{:S(2)}) async-start(), calls=%async_computation.2 | async-start | bytes 3538944 | tf_op jit(solution)/shard_map/all_gather | solution.py:189
  12.8 41.0 %copy-start.68 = (f32[4]{0:T(128)}, f32[4]{0:T(128)S(1)}, u32[]{:S(2)}) copy-start(f32[4]{0:T(128)S(1)} %get-tuple-element.304) | copy-start | bytes 52
  12.8 10.8 copy-start.34
  16.4 34.2 %copy-start.40 = (f32[5120]{0:T(1024)S(1)}, f32[5120]{0:T(1024)}, u32[]{:S(2)}) copy-start(f32[5120]{0:T(1024)} %param.47) | copy-start | bytes 61444
  17.3 39.2 %collective-permute-start.1 = (bf16[1,196,1024]{2,1,0:T(8,128)(2,1)}, bf16[1,196,1024]{2,1,0:T(8,128)(2,1)}, u32[]{:S(2)}, u32[]{:S(2)}) collective-permute-start(bf16[1,196,1024]{2,1,0:T(8,128)(2,1)} %get-tuple-element.308), channel_id=1, source_target_pairs={{1,0},{2,1},{3,2},{4,3},{5,4},{6,5},{7,6},{9,8},{10,9},{11,10},{12... | collective-permute-start | bytes 1204232 | tf_op jit(solution)/shard_map/ppermute | solution.py:41
  18.6 39.0 %collective-permute-start = (bf16[1,196,1024]{2,1,0:T(8,128)(2,1)}, bf16[1,196,1024]{2,1,0:T(8,128)(2,1)}, u32[]{:S(2)}, u32[]{:S(2)}) collective-permute-start(bf16[1,196,1024]{2,1,0:T(8,128)(2,1)} %get-tuple-element.307), channel_id=1, source_target_pairs={{0,1},{1,2},{2,3},{3,4},{4,5},{5,6},{6,7},{8,9},{9,10},{10,11},{11... | collective-permute-start | bytes 1204232 | tf_op jit(solution)/shard_map/ppermute | solution.py:39
  22.7 29.1 %copy-start.16 = (f32[128,3,512]{0,2,1:T(8,128)}, f32[128,3,512]{0,2,1:T(8,128)S(1)}, u32[]{:S(2)}) copy-start(f32[128,3,512]{0,2,1:T(8,128)S(1)} %copy.127) | copy-start | bytes 2359300
  23.6 637.6 %all-gather.11.cloned.1.call-start = ((), (), s32[]{:S(2)}) async-start(), calls=%async_computation.3 | async-start | bytes 1179648 | tf_op jit(solution)/shard_map/all_gather | solution.py:190
  51.7 64.5 %copy-start.54 = (f32[256]{0:T(256)}, f32[256]{0:T(256)S(1)}, u32[]{:S(2)}) copy-start(f32[256]{0:T(256)S(1)} %get-tuple-element.328) | copy-start | bytes 3076
  51.7 64.5 %copy-start.57 = (f32[256]{0:T(256)}, f32[256]{0:T(256)S(1)}, u32[]{:S(2)}) copy-start(f32[256]{0:T(256)S(1)} %get-tuple-element.327) | copy-start | bytes 3076
  53.9 62.3 %copy-start.35 = (f32[784]{0:T(1024)}, f32[784]{0:T(1024)S(1)}, u32[]{:S(2)}) copy-start(f32[784]{0:T(1024)S(1)} %mul.739) | copy-start | bytes 9412
  73.0 60.7 %copy-start.9 = (f32[784,256]{1,0:T(8,128)}, f32[784,256]{1,0:T(8,128)S(1)}, u32[]{:S(2)}) copy-start(f32[784,256]{1,0:T(8,128)S(1)} %get-tuple-element.337) | copy-start | bytes 2408452
  127.0 6.7 copy-start.36
  127.0 6.7 copy-start.49
  127.0 6.6 copy-start.52
  127.0 6.6 copy-start.55
  127.0 6.6 copy-start.58
  137.8 45.5 %copy-start.74 = (f32[256]{0:T(256)S(1)}, f32[256]{0:T(256)}, u32[]{:S(2)}) copy-start(f32[256]{0:T(256)} %get-tuple-element.325) | copy-start | bytes 3076
  137.8 45.5 %copy-start.76 = (f32[256]{0:T(256)S(1)}, f32[256]{0:T(256)}, u32[]{:S(2)}) copy-start(f32[256]{0:T(256)} %get-tuple-element.326) | copy-start | bytes 3076
  183.3 43.5 %copy-start.5 = (f32[784,1024]{1,0:T(8,128)S(1)}, f32[784,1024]{1,0:T(8,128)}, u32[]{:S(2)}) copy-start(f32[784,1024]{1,0:T(8,128)} %reshape.575) | copy-start | bytes 9633796
  183.3 43.5 %copy-start.46 = (f32[1024]{0:T(1024)S(1)}, f32[1024]{0:T(1024)}, u32[]{:S(2)}) copy-start(f32[1024]{0:T(1024)} %get-tuple-element.323) | copy-start | bytes 12292
  183.4 43.5 %copy-start.64 = (f32[1024]{0:T(1024)S(1)}, f32[1024]{0:T(1024)}, u32[]{:S(2)}) copy-start(f32[1024]{0:T(1024)} %get-tuple-element.322) | copy-start | bytes 12292
  226.8 4.9 copy-start.42
  226.8 4.8 copy-start.44
  238.8 3.7 collective-permute-start.2
  245.8 72.1 %collective-permute-start.3 = (bf16[1568,1024]{1,0:T(8,128)(2,1)S(1)}, bf16[1568,1024]{1,0:T(8,128)(2,1)}, u32[]{:S(2)}, u32[]{:S(2)}) collective-permute-start(bf16[1568,1024]{1,0:T(8,128)(2,1)S(1)} %maximum_select_fusion.2), channel_id=1, source_target_pairs={{0,2},{1,3},{2,0},{3,1},{4,6},{5,7},{6,4},{7,5},{8,10},{9,11},{10,... | collective-permute-start | bytes 9633800 | tf_op jit(solution)/shard_map/ppermute | solution.py:28
  248.0 79.7 %copy-start.27 = (f32[64,1024]{1,0:T(8,128)S(1)}, f32[64,1024]{1,0:T(8,128)}, u32[]{:S(2)}) copy-start(f32[64,1024]{1,0:T(8,128)} %param.46) | copy-start | bytes 786436
  325.1 287.2 %collective-permute-start.4 = (bf16[3136,1024]{1,0:T(8,128)(2,1)}, bf16[3136,1024]{1,0:T(8,128)(2,1)}, u32[]{:S(2)}, u32[]{:S(2)}) collective-permute-start(bf16[3136,1024]{1,0:T(8,128)(2,1)} %maximum_select_fusion.1), channel_id=1, source_target_pairs={{0,4},{1,5},{2,6},{3,7},{4,0},{5,1},{6,2},{7,3},{8,12},{9,13},{10,... | collective-permute-start | bytes 19267592 | tf_op jit(solution)/shard_map/ppermute | solution.py:28
  328.4 1335.7 %all-reduce.13.cloned.1.call-start = ((), (), s32[]{:S(2)}) async-start(), calls=%async_computation.4 | async-start | bytes 29884416 | tf_op jit(solution)/shard_map/psum | solution.py:328
  624.4 12.3 copy-start.4
  703.9 44.3 %copy-start.66 = (f32[1024]{0:T(1024)S(1)}, f32[1024]{0:T(1024)}, u32[]{:S(2)}) copy-start(f32[1024]{0:T(1024)} %get-tuple-element.321) | copy-start | bytes 12292
  703.9 44.3 %copy-start.67 = (f32[1024]{0:T(1024)S(1)}, f32[1024]{0:T(1024)}, u32[]{:S(2)}) copy-start(f32[1024]{0:T(1024)} %get-tuple-element.324) | copy-start | bytes 12292
  748.2 4.9 copy-start.60
  748.2 4.9 copy-start.62
  748.2 6.0 copy-start.80
  785.4 33.9 %copy-start.1 = (f32[6272,512]{1,0:T(8,128)}, f32[6272,512]{1,0:T(8,128)S(1)}, u32[]{:S(2)}) copy-start(f32[6272,512]{1,0:T(8,128)S(1)} %fusion.3) | copy-start | bytes 38535172
  828.3 277.7 %collective-permute-start.5 = (bf16[3136,1024]{1,0:T(8,128)(2,1)}, bf16[3136,1024]{1,0:T(8,128)(2,1)}, u32[]{:S(2)}, u32[]{:S(2)}) collective-permute-start(bf16[3136,1024]{1,0:T(8,128)(2,1)} %select_convert_fusion), channel_id=1, source_target_pairs={{0,4},{1,5},{2,6},{3,7},{4,0},{5,1},{6,2},{7,3},{8,12},{9,13},{10,... | collective-permute-start | bytes 19267592 | tf_op jit(solution)/shard_map/ppermute | solution.py:28
  1124.5 71.7 %collective-permute-start.6 = (bf16[1568,1024]{1,0:T(8,128)(2,1)}, bf16[1568,1024]{1,0:T(8,128)(2,1)}, u32[]{:S(2)}, u32[]{:S(2)}) collective-permute-start(bf16[1568,1024]{1,0:T(8,128)(2,1)} %select_convert_fusion.1), channel_id=1, source_target_pairs={{0,2},{1,3},{2,0},{3,1},{4,6},{5,7},{6,4},{7,5},{8,10},{9,11},{10,... | collective-permute-start | bytes 9633800 | tf_op jit(solution)/shard_map/ppermute | solution.py:28
  1204.0 10.2 collective-permute-start.7
  1216.0 5.5 copy-start.6
  1216.1 5.5 copy-start.7
  1216.1 5.5 copy-start.43
  1216.1 5.5 copy-start.45
  1216.1 5.5 copy-start.47
  1216.1 5.5 copy-start.65
  1216.1 5.5 copy-start.79
  1314.2 5.1 copy-start.25
  1396.3 6.2 copy-start.19
  1406.0 5.6 copy-start.63
  1406.0 5.6 copy-start.61
  1408.8 3.3 collective-permute-start.9
  1410.1 5.1 collective-permute-start.8
  1411.6 9.1 copy-start.41
  1669.0 9.7 copy-start.3
  1675.8 5.3 copy-start.14
  1692.1 10.4 copy-start.24
  1696.7 5.8 copy-start.37
  1696.7 8.0 copy-start.15
  1696.7 8.0 copy-start.28
  1696.7 8.0 copy-start.38
  1696.7 8.0 copy-start.39
  (32 other events, 88.1 us)
Sparse Core Ops, SparseCore 0:
  10.2 33.2 all-gather.4
  45.7 22.9 all-gather.6
  70.8 39.9 all-gather.8
  328.5 285.3 all-gather.10
  1402.7 261.3 all-reduce.12
where the time goes:
time: 1730 us; the launch traced here: 1720 us
  waiting for transfers between devices  918 us (53%)
  blocking collectives  350 us (20%)
  other arithmetic  163 us (9%)
  matrix products  136 us (8%)
  local copies, waits for them, and re-layouts  118 us (7%)
  between operations  21.4 us (1%)
    ppermute x6, waiting for transfers between devices, swapped(): return lax.ppermute(value, axis, pairs)  676 us
    psum x1, waiting for transfers between devices, body(): lax.psum((local_terms[0], local_terms[1], local_terms[2], local_terms[3],...  239 us
    psum x4, blocking collectives, batch_stats(): lax.psum((jnp.sum(values * valid_rows, axis=0), jnp.sum(values * values *...  162 us
    psum x4, blocking collectives, batch_back(): lax.psum((jnp.sum(incoming, axis=0), jnp.sum(incoming * normal, axis=0)),...  161 us
    unnamed x189, local copies, waits for them, and re-layouts  55 us
  transfers between devices with their start and end apart: 15, of which 7 were waited for; matrix products, arithmetic and copies ran while one was open for 10% of the time, Pallas kernels for 0%

commit v1 on v0

--- a/solution.py
+++ b/solution.py
@@ -20,12 +20,6 @@
 CLIP_AT = 1.0
 GAIN_RATE = 0.5
 MASKED = -1e30
-
-
-def swapped(value, axis, apart):
-    mask = 2**apart
-    pairs = [(source, source ^ mask) for source in range(lax.axis_size(axis))]
-    return lax.ppermute(value, axis, pairs)
 
 
 def with_halo(cells, sides, width):
@@ -46,9 +40,10 @@
 
 
 def batch_stats(values, valid_rows, row_total):
-    sums = lax.psum(
-        (jnp.sum(values * valid_rows, axis=0), jnp.sum(values * values * valid_rows, axis=0)),
-        ("clip", "chan"),
+    sums = total(
+        jnp.stack(
+            [jnp.sum(values * valid_rows, axis=0), jnp.sum(values * values * valid_rows, axis=0)]
+        )
     )
     mean = sums[0] / row_total
     scales = lax.rsqrt(sums[1] / row_total - mean * mean + EPS_NORM)
@@ -56,9 +51,7 @@
 
 
 def batch_back(incoming, normal, scales, gains, valid_rows, row_total):
-    sums = lax.psum(
-        (jnp.sum(incoming, axis=0), jnp.sum(incoming * normal, axis=0)), ("clip", "chan")
-    )
+    sums = total(jnp.stack([jnp.sum(incoming, axis=0), jnp.sum(incoming * normal, axis=0)]))
     removed = (sums[0] + normal * sums[1]) / row_total
     return (valid_rows * gains * scales * (incoming - removed), sums[1], sums[0])
 
@@ -98,30 +91,23 @@
     return padded[:, 1:-1, 1:-1].reshape(frames * HH * WW, channels)
 
 
-def gather_clip(pairs, chan_at):
-    current = pairs
-    for level in range(DPC.bit_length() - 1):
-        partner = swapped(current, "chan", level)
-        lower = chan_at >> level & 1 == 0
-        current = jnp.where(
-            lower,
-            jnp.concatenate([current, partner], axis=0),
-            jnp.concatenate([partner, current], axis=0),
-        )
-    return current
-
-
-def sum_clip(pairs, chan_at):
-    current = pairs
-    for level in reversed(range(DPC.bit_length() - 1)):
-        half_rows = current.shape[0] // 2
-        lower = chan_at >> level & 1 == 0
-        kept = jnp.where(lower, current[:half_rows], current[half_rows:])
-        outgoing = jnp.where(lower, current[half_rows:], current[:half_rows])
-        current = kept + swapped(outgoing.astype(jnp.bfloat16), "chan", level).astype(
-            outgoing.dtype
-        )
-    return current
+def flipped(value, axis, mask):
+    pairs = [(source, source ^ mask) for source in range(lax.axis_size(axis))]
+    return lax.ppermute(value, axis, pairs)
+
+
+def total(value):
+    for axis in ("chan", "clip"):
+        bits = lax.axis_size(axis).bit_length() - 1
+        levels = list(range(bits))
+        groups = [levels[:1]] if axis == "chan" else []
+        rest = levels[len(groups) :]
+        groups += [rest[index : index + 2] for index in range(0, len(rest), 2)]
+        for group in groups:
+            base = 1 << group[0]
+            parts = [flipped(value, axis, base * turn) for turn in range(1, 1 << len(group))]
+            value = value + sum(parts[1:], parts[0])
+    return value
 
 
 def adam_step(master, gradient, moment, second, factor, rate):
@@ -173,9 +159,10 @@
     frame_ok = (local_frames < length).astype(jnp.float32)
     valid_rows = jnp.repeat(frame_ok, spot_count)[:, None]
     row_total = jnp.sum(frame_counts).astype(jnp.float32) * spot_count
-    key_ok = jnp.repeat(
-        (jnp.arange(DPC * frames, dtype=jnp.int32) < length).astype(jnp.float32), spot_count
-    )
+    block_frames = jnp.concatenate(
+        [(clip_place ^ turn) * frames + jnp.arange(frames, dtype=jnp.int32) for turn in range(4)]
+    )
+    key_ok = jnp.repeat((block_frames < length).astype(jnp.float32), spot_count)
     span_list = [narrow] * 4 + [model_width] * 4
     starts = [sum(span_list[:index]) for index in range(8)]
     pieces = [norm_params[starts[index] : starts[index] + span_list[index]] for index in range(8)]
@@ -220,56 +207,103 @@
         preferred_element_type=jnp.float32,
     ).astype(jnp.bfloat16)
     query = projected[:, :inner_width]
-    clip_pairs = gather_clip(projected[:, inner_width:], chan_at)
+    pair_own = projected[:, inner_width:]
+    pair_far = flipped(pair_own, "chan", 2)
+    query_far = flipped(query, "chan", 4)
+    clip_pairs = jnp.concatenate(
+        [pair_own, flipped(pair_own, "chan", 1), pair_far, flipped(pair_far, "chan", 1)], axis=0
+    )
     keys_all = clip_pairs[:, :inner_width]
     values_all = clip_pairs[:, inner_width:]
     scaling = inner_width ** (-0.5)
-    scores = jnp.einsum("qd,kd->qk", query, keys_all, preferred_element_type=jnp.float32) * scaling
-    scores = jnp.where(key_ok[None, :] > 0, scores, MASKED)
-    row_peak = jnp.max(scores, axis=1, keepdims=True)
-    lifted = jnp.exp(scores - row_peak) * key_ok[None, :]
-    row_sums = jnp.sum(lifted, axis=1, keepdims=True)
-    weights = lifted / row_sums
-    log_total = row_peak + jnp.log(row_sums)
-    attended = jnp.dot(
-        weights.astype(jnp.bfloat16), values_all, preferred_element_type=jnp.float32
-    ).astype(jnp.bfloat16)
+
+    def attend(rows):
+        scores = (
+            jnp.einsum("qd,kd->qk", rows, keys_all, preferred_element_type=jnp.float32) * scaling
+        )
+        scores = jnp.where(key_ok[None, :] > 0, scores, MASKED)
+        row_peak = jnp.max(scores, axis=1, keepdims=True)
+        lifted = jnp.exp(scores - row_peak)
+        row_sums = jnp.sum(lifted, axis=1, keepdims=True)
+        weights = lifted / row_sums
+        part = jnp.dot(
+            weights.astype(jnp.bfloat16), values_all, preferred_element_type=jnp.float32
+        )
+        return part, row_peak + jnp.log(row_sums)
+
+    part_far, log_far = attend(query_far)
+    part_far = flipped(part_far.astype(jnp.bfloat16), "chan", 4).astype(jnp.float32)
+    log_far = flipped(log_far, "chan", 4)
+    part_own, log_own = attend(query)
+    log_peak = jnp.maximum(log_own, log_far)
+    log_total = log_peak + jnp.log(jnp.exp(log_own - log_peak) + jnp.exp(log_far - log_peak))
+    attended_wide = part_own * jnp.exp(log_own - log_total) + part_far * jnp.exp(log_far - log_total)
+    attended = attended_wide.astype(jnp.bfloat16)
     attn_pre = jnp.dot(attended, back_low, preferred_element_type=jnp.float32)
-    normal_four, scale_four = batch_stats(attn_pre, valid_rows, row_total)
+    outer_grad = cotangent.reshape(row_count, model_width).astype(jnp.float32) * valid_rows
+    sums = total(
+        jnp.stack(
+            [
+                jnp.sum(attn_pre * valid_rows, axis=0),
+                jnp.sum(attn_pre * attn_pre * valid_rows, axis=0),
+                jnp.sum(outer_grad, axis=0),
+                jnp.sum(outer_grad * attn_pre, axis=0),
+            ]
+        )
+    )
+    mean_four = sums[0] / row_total
+    scale_four = lax.rsqrt(sums[1] / row_total - mean_four * mean_four + EPS_NORM)
+    normal_four = (attn_pre - mean_four) * scale_four
+    shift_four_grad = sums[2]
+    gain_four_grad = scale_four * (sums[3] - mean_four * sums[2])
     mixed = (
         ((residual_out + (normal_four * gain_four + shift_four)) * valid_rows)
         .astype(jnp.bfloat16)
         .reshape(frames, spot_count, model_width)
     )
-    outer_grad = cotangent.reshape(row_count, model_width).astype(jnp.float32) * valid_rows
-    attn_grad, gain_four_grad, shift_four_grad = batch_back(
-        outer_grad, normal_four, scale_four, gain_four, valid_rows, row_total
-    )
-    attn_grad = attn_grad.astype(jnp.bfloat16)
+    removed_four = (shift_four_grad + normal_four * gain_four_grad) / row_total
+    attn_grad = (valid_rows * gain_four * scale_four * (outer_grad - removed_four)).astype(
+        jnp.bfloat16
+    )
     back_local = jnp.einsum("rd,re->de", attended, attn_grad, preferred_element_type=jnp.float32)
     attended_grad = jnp.einsum(
         "re,de->rd", attn_grad, back_low, preferred_element_type=jnp.float32
     ).astype(jnp.bfloat16)
-    again = jnp.einsum("qd,kd->qk", query, keys_all, preferred_element_type=jnp.float32) * scaling
-    again = jnp.where(key_ok[None, :] > 0, again, MASKED)
-    weights = jnp.exp(again - log_total) * key_ok[None, :]
-    prob_grad = jnp.einsum(
-        "qd,kd->qk", attended_grad, values_all, preferred_element_type=jnp.float32
-    )
-    row_term = jnp.sum(weights * prob_grad, axis=1, keepdims=True)
-    score_grad = (weights * (prob_grad - row_term)).astype(jnp.bfloat16)
+    row_term = jnp.sum(attended_grad.astype(jnp.float32) * attended_wide, axis=1, keepdims=True)
+    attended_grad_far = flipped(attended_grad, "chan", 4)
+    terms_far = flipped(jnp.concatenate([log_total, row_term], axis=1), "chan", 4)
+
+    def attend_back(rows, rows_grad, logs, terms):
+        again = jnp.einsum("qd,kd->qk", rows, keys_all, preferred_element_type=jnp.float32) * scaling
+        again = jnp.where(key_ok[None, :] > 0, again, MASKED)
+        weights = jnp.exp(again - logs)
+        prob_grad = jnp.einsum(
+            "qd,kd->qk", rows_grad, values_all, preferred_element_type=jnp.float32
+        )
+        score_grad = (weights * (prob_grad - terms)).astype(jnp.bfloat16)
+        rows_back = jnp.dot(score_grad, keys_all, preferred_element_type=jnp.float32) * scaling
+        key_part = (
+            jnp.einsum("qk,qd->kd", score_grad, rows, preferred_element_type=jnp.float32) * scaling
+        )
+        value_part = jnp.einsum(
+            "qk,qd->kd",
+            weights.astype(jnp.bfloat16),
+            rows_grad,
+            preferred_element_type=jnp.float32,
+        )
+        return rows_back, jnp.concatenate([key_part, value_part], axis=1)
+
+    query_own, pair_grad_own = attend_back(query, attended_grad, log_total, row_term)
+    query_part, pair_grad_far = attend_back(
+        query_far, attended_grad_far, terms_far[:, :1], terms_far[:, 1:]
+    )
     query_grad = (
-        jnp.dot(score_grad, keys_all, preferred_element_type=jnp.float32) * scaling
+        query_own + flipped(query_part.astype(jnp.bfloat16), "chan", 4).astype(jnp.float32)
     ).astype(jnp.bfloat16)
-    key_grad = (
-        jnp.einsum("qk,qd->kd", score_grad, query, preferred_element_type=jnp.float32) * scaling
-    )
-    value_grad = jnp.einsum(
-        "qk,qd->kd", weights.astype(jnp.bfloat16), attended_grad, preferred_element_type=jnp.float32
-    )
-    pair_grad = sum_clip(jnp.concatenate([key_grad, value_grad], axis=1), chan_at).astype(
-        jnp.bfloat16
-    )
+    pair_sum = (pair_grad_own + pair_grad_far).reshape(4, row_count, 2 * inner_width)
+    near = flipped(pair_sum[1::2].astype(jnp.bfloat16), "chan", 1).astype(jnp.float32)
+    far = flipped((pair_sum[2] + near[1]).astype(jnp.bfloat16), "chan", 2).astype(jnp.float32)
+    pair_grad = (pair_sum[0] + near[0] + far).astype(jnp.bfloat16)
     projected_grad = jnp.concatenate([query_grad, pair_grad], axis=1)
     embed_local = jnp.einsum(
         "rd,re->de", residual_low, projected_grad, preferred_element_type=jnp.float32
@@ -325,10 +359,10 @@
         .reshape(frames, spot_count, model_width)
     )
     local_terms = (first_local, middle_local, last_local, embed_local, back_local)
-    summed = lax.psum(
-        (local_terms[0], local_terms[1], local_terms[2], local_terms[3], local_terms[4]),
-        ("clip", "chan"),
-    )
+    summed = [
+        lax.psum(item.astype(jnp.bfloat16), ("clip", "chan")).astype(jnp.float32)
+        for item in local_terms[:4]
+    ] + [lax.psum(local_terms[4], ("clip", "chan"))]
     norm_gradient = jnp.concatenate(
         [
             gain_one_grad,

time: 1730 us -> 886 us (0.51)
  waiting for transfers between devices: 918 us -> 401 us
  blocking collectives: 350 us -> 15.8 us
  starting transfers between devices: 13.8 us -> 82.6 us
  other arithmetic: 163 us -> 106 us
    ppermute x6 -> x60, waiting for transfers between devices: 676 us -> 195 us  [flipped(): return lax.ppermute(value, axis, pairs)]
    psum x8 -> x0, blocking collectives: 323 us -> none  [the longest x4 162 us: batch_stats(): lax.psum((jnp.sum(values * valid_rows, axis=0), jnp.sum(values * values *...]
    ppermute x6 -> x60, starting transfers between devices: 5.54 us -> 74.6 us  [flipped(): return lax.ppermute(value, axis, pairs)]
    psum x1 -> x2, waiting for transfers between devices: 239 us -> 194 us  [the longest x1 139 us: body(): lax.psum(item.astype(jnp.bfloat16), ('clip', 'chan')).astype(jnp.float32)]
    select_n x3 -> x0, other arithmetic: 22.6 us -> none  [gather_clip(): jnp.where(lower, jnp.concatenate([current, partner], axis=0), jnp.concate...]
    add x3 -> x26, other arithmetic: 19.2 us -> 0.33 us  [the longest x21 0.25 us: total(): value = value + sum(parts[1:], parts[0])]
    convert_element_type x7 -> x6, other arithmetic: 36.7 us -> 18.8 us  [the longest x1 5.38 us: body(): pair_grad = (pair_sum[0] + near[0] + far).astype(jnp.bfloat16)]
    unnamed x189 -> x245, local copies, waits for them, and re-layouts: 55 us -> 37.5 us
  transfers between devices with their start and end apart: 15 -> 70, of which waited for: 7 -> 37; matrix products, arithmetic and copies ran while one was open for 10% -> 26% of each run, Pallas kernels for 0% -> 0%
where the time goes in v1:
time: 886 us; the launch traced here: 876 us
  waiting for transfers between devices  401 us (45%)
  matrix products  130 us (15%)
  local copies, waits for them, and re-layouts  118 us (13%)
  other arithmetic  106 us (12%)
  starting transfers between devices  82.6 us (9%)
  between operations  22.1 us (2%)
  blocking collectives  15.8 us (2%)
    ppermute x60, waiting for transfers between devices, flipped(): return lax.ppermute(value, axis, pairs)  195 us
    psum x1, waiting for transfers between devices, body(): lax.psum(item.astype(jnp.bfloat16), ('clip', 'chan')).astype(jnp.float32)  139 us
    ppermute x60, starting transfers between devices, flipped(): return lax.ppermute(value, axis, pairs)  74.6 us
    psum x1, waiting for transfers between devices, body(): lax.psum(local_terms[4], ('clip', 'chan'))  54.4 us
    unnamed x245, local copies, waits for them, and re-layouts  37.5 us
  transfers between devices with their start and end apart: 70, of which 37 were waited for; matrix products, arithmetic and copies ran while one was open for 26% of the time, Pallas kernels for 0%

profile of v1, /device:TPU:0, one launch (start us, length us, event | category | flops | bytes accessed | tf_op | source)
XLA Modules:
  0.0 876.1 jit_solution(8725529793790617035)
XLA Ops:
  15.5 3.8 collective-permute-start
  21.1 5.2 fusion.13
  26.2 4.5 reshape.580
  30.7 9.4 %all-gather.5.cloned.1.call-done = bf16[3,1024,256]{2,1,0:T(8,128)(2,1)} async-done(((bf16[3,128,256]{2,1,0:T(8,128)(2,1)}), bf16[3,1024,256]{2,1,0:T(8,128)(2,1)}) %all-gather.5.cloned.1.call-update) | async-done | bytes 1572880 | tf_op jit(solution)/shard_map/all_gather | solution.py:173
  40.1 4.3 multiply_reduce_fusion.18
  44.5 5.0 collective-permute-start.2
  50.4 5.2 collective-permute-start.3
  55.6 4.1 collective-permute-start.4
  61.2 3.8 collective-permute-done.5
  73.7 5.1 pad_slice_fusion
  99.3 3.6 multiply_reduce_fusion.16
  104.8 3.8 collective-permute-start.12
  113.8 15.8 %all_gather.17 = bf16[256,1024]{1,0:T(8,128)(2,1)S(1)} all-gather(bf16[32,1024]{1,0:T(8,128)(2,1)S(1)} %convert_element_type.183), channel_id=1, replica_groups=mesh['clip'=4,'chan'=8] {'chan'}, dimensions={0}, use_global_device_ids=true | all-gather | bytes 589824 | tf_op jit(solution)/shard_map/all_gather | solution.py:175
  139.7 3.3 collective-permute-done.19
  149.3 4.1 multiply_multiply_fusion.1
  153.4 5.9 convolution_convert_fusion.1
  161.3 35.1 %collective-permute-done.24 = bf16[784,1024]{1,0:T(8,128)(2,1)} collective-permute-done((bf16[784,1024]{1,0:T(8,128)(2,1)}, bf16[784,1024]{1,0:T(8,128)(2,1)}, u32[]{:S(2)}, u32[]{:S(2)}) %collective-permute-start.24) | collective-permute-done | bytes 1605664 | tf_op jit(solution)/shard_map/ppermute | solution.py:96
  205.8 4.1 pad_maximum_fusion
  209.9 5.1 fusion.103
  215.0 34.0 %collective-permute-done.26 = bf16[784,512]{1,0:T(8,128)(2,1)S(1)} collective-permute-done((bf16[784,512]{1,0:T(8,128)(2,1)S(1)}, bf16[784,512]{1,0:T(8,128)(2,1)S(1)}, u32[]{:S(2)}, u32[]{:S(2)}) %collective-permute-start.26) | collective-permute-done | bytes 802848 | tf_op jit(solution)/shard_map/ppermute | solution.py:96
  249.1 3.4 fusion.102
  256.2 4.8 fusion.35
  265.6 17.0 %collective-permute-done.27 = f32[784,1]{0,1:T(1,128)S(1)} collective-permute-done((f32[784,1]{0,1:T(1,128)S(1)}, f32[784,1]{0,1:T(1,128)S(1)}, u32[]{:S(2)}, u32[]{:S(2)}) %collective-permute-start.27) | collective-permute-done | bytes 3168 | tf_op jit(solution)/shard_map/ppermute | solution.py:96
  282.6 16.7 %collective-permute-done.28 = bf16[784,512]{1,0:T(8,128)(2,1)S(1)} collective-permute-done((bf16[784,512]{1,0:T(8,128)(2,1)S(1)}, bf16[784,512]{1,0:T(8,128)(2,1)S(1)}, u32[]{:S(2)}, u32[]{:S(2)}) %collective-permute-start.28) | collective-permute-done | bytes 802848 | tf_op jit(solution)/shard_map/ppermute | solution.py:96
  300.2 4.8 fusion.46
  304.9 3.0 multiply_reduce_fusion.5
  310.7 3.0 collective-permute-start.32
  324.4 2.9 multiply_convert_fusion.3
  328.7 6.9 multiply_convert_fusion.1
  335.6 7.3 fusion.7
  343.0 2.9 collective-permute-start.36
  345.9 6.2 convolution_multiply_fusion.1
  352.1 11.5 %collective-permute-done.36 = f32[784,2]{0,1:T(2,128)S(1)} collective-permute-done((f32[784,2]{0,1:T(2,128)S(1)}, f32[784,2]{0,1:T(2,128)S(1)}, u32[]{:S(2)}, u32[]{:S(2)}) %collective-permute-start.36) | collective-permute-done | bytes 6304 | tf_op jit(solution)/shard_map/ppermute | solution.py:96
  364.6 5.1 fusion.5
  369.7 10.3 %multiply_convert_fusion = bf16[784,3136]{1,0:T(8,128)(2,1)} fusion(f32[784,3136]{1,0:T(8,128)} %copy-done.9, bf16[784,512]{1,0:T(8,128)(2,1)} %copy-done.101, f32[784]{0:T(1024)S(1)} %get-tuple-element.231, f32[784]{0:T(1024)S(1)} %get-tuple-element.232, bf16[3136,1024]{1,0:T(8,128)(2,1)} %copy-done.14), kind=kOutput, calls=%fused_computation.2 | convolution fusion | flops 2527465472 | bytes 18972800 | tf_op jit(solution)/shard_map/qd,kd->qk/dot_general | solution.py:280
  380.0 9.1 %convolution_multiply_fusion = f32[3136,512]{1,0:T(8,128)} fusion(bf16[784,3136]{1,0:T(8,128)(2,1)} %multiply_convert_fusion, bf16[784,512]{1,0:T(8,128)(2,1)} %copy-done.98), kind=kOutput, calls=%fused_computation.16 | convolution fusion | flops 2519236608 | bytes 12142592 | tf_op jit(solution)/shard_map/qk,qd->kd/dot_general | solution.py:286
  389.1 7.7 fusion
  399.1 5.7 collective-permute-done.39
  404.8 3.5 convert_element_type.208
  408.3 3.3 fusion.16
  411.6 6.3 multiply_convert_fusion.5
  419.7 5.7 fusion.29
  425.4 38.3 %collective-permute-done.38 = bf16[784,512]{1,0:T(8,128)(2,1)S(1)} collective-permute-done((bf16[784,512]{1,0:T(8,128)(2,1)S(1)}, bf16[784,512]{1,0:T(8,128)(2,1)S(1)}, u32[]{:S(2)}, u32[]{:S(2)}) %collective-permute-start.38) | collective-permute-done | bytes 802848 | tf_op jit(solution)/shard_map/ppermute | solution.py:96
  466.1 5.4 fusion.20
  471.5 9.5 %fusion.81 = (f32[1024]{0:T(1024)S(1)}, f32[1024]{0:T(1024)S(1)}, f32[784,1024]{1,0:T(8,128)S(1)}) fusion(f32[1024]{0:T(1024)S(1)} %bitcast.193, f32[784,1024]{1,0:T(8,128)} %get-tuple-element.320, f32[1024]{0:T(1024)S(1)} %bitcast.196, f32[784,1024]{1,0:T(8,128)} %reshape.601, f32[1024]{0:T(1024)S(1)} %copy-done.86, f32[1024]{0:T(1024)S(1)} %copy-done.72, ...), kind=kOutput, calls=%fused_computation.266 | convolution fusion | flops 2486319104 | bytes 18426944 | tf_op jit(solution)/shard_map/re,de->rd/dot_general | solution.py:311
  500.2 3.0 collective-permute-start.50
  505.0 7.5 copy.101
  512.6 6.4 copy.103
  522.5 3.7 fusion.104
  529.5 3.1 copy-done
  534.0 3.2 scatter-add.31
  537.3 3.3 add_select_fusion
  540.6 3.0 scatter-add.34
  568.5 6.5 convolution_convert_fusion
  575.0 5.2 copy.105
  580.3 3.1 collective-permute-start.57
  596.5 3.0 convolution_convert_fusion.2
  605.7 54.4 %all-reduce.6.cloned.1.call-done = f32[512,1024]{1,0:T(8,128)} async-done(((f32[512,1024]{1,0:T(8,128)}), f32[512,1024]{1,0:T(8,128)}) %all-reduce.6.cloned.1.call-update) | async-done | bytes 2097168 | tf_op jit(solution)/shard_map/psum | solution.py:365
  677.6 4.4 fusion.22
  686.1 139.4 %all-reduce.8.cloned.1.call-done = (bf16[3,1024,256]{2,1,0:T(8,128)(2,1)}, bf16[9,256,256]{2,1,0:T(8,128)(2,1)}, bf16[256,1024]{1,0:T(8,128)(2,1)}, bf16[1024,3,512]{0,2,1:T(8,128)(2,1)}) async-done(((bf16[3,1024,256]{2,1,0:T(8,128)(2,1)}, bf16[9,256,256]{2,1,0:T(8,128)(2,1)}, bf16[256,1024]{1,0:T(8,128)(2,1)}, bf16[1024,3,512]{0,2,1:T(8,128)(2,1)}), (bf16[3,1024,256]{2,1,0:T(8,128)(2,1)}, ...) | async-done | bytes 6422544 | tf_op jit(solution)/shard_map/psum | solution.py:363
  825.5 4.3 multiply_reduce_fusion
  829.8 3.5 convert_element_type.224
  833.2 3.7 copy.112
  836.9 4.5 multiply_reduce_fusion.8
  (512 shorter events, 223.3 us)
Async XLA Ops:
  7.2 32.9 %all-gather.5.cloned.1.call-start = ((), (), s32[]{:S(2)}) async-start(), calls=%async_computation | async-start | bytes 1769472 | tf_op jit(solution)/shard_map/all_gather | solution.py:173
  9.0 90.3 %all-gather.7.cloned.1.call-start = ((), (), s32[]{:S(2)}) async-start(), calls=%async_computation.1 | async-start | bytes 1327104 | tf_op jit(solution)/shard_map/all_gather | solution.py:174
  13.5 6.0 collective-permute-start.1
  15.5 137.9 %all-gather.9.cloned.1.call-start = ((), (), s32[]{:S(2)}) async-start(), calls=%async_computation.2 | async-start | bytes 3538944 | tf_op jit(solution)/shard_map/all_gather | solution.py:176
  15.5 4.5 collective-permute-start
  44.5 5.8 collective-permute-start.2
  50.4 10.5 %collective-permute-start.3 = (f32[2,256]{1,0:T(2,128)S(1)}, f32[2,256]{1,0:T(2,128)S(1)}, u32[]{:S(2)}, u32[]{:S(2)}) collective-permute-start(f32[2,256]{1,0:T(2,128)S(1)} %fusion.74), channel_id=1, source_target_pairs={{0,2},{1,3},{2,0},{3,1},{4,6},{5,7},{6,4},{7,5},{8,10},{9,11},{10,... | collective-permute-start | bytes 6152 | tf_op jit(solution)/shard_map/ppermute | solution.py:96
  55.6 5.7 collective-permute-start.4
  59.6 5.4 collective-permute-start.5
  60.8 244.1 %all-gather.11.cloned.1.call-start = ((), (), s32[]{:S(2)}) async-start(), calls=%async_computation.3 | async-start | bytes 1179648 | tf_op jit(solution)/shard_map/all_gather | solution.py:177
  65.0 4.3 collective-permute-start.6
  66.6 3.6 collective-permute-start.7
  68.0 4.5 collective-permute-start.8
  104.2 4.5 collective-permute-start.10
  104.3 4.5 collective-permute-start.11
  104.8 5.4 collective-permute-start.12
  110.2 19.4 %collective-permute-start.13 = (f32[2,256]{1,0:T(2,128)S(1)}, f32[2,256]{1,0:T(2,128)S(1)}, u32[]{:S(2)}, u32[]{:S(2)}) collective-permute-start(f32[2,256]{1,0:T(2,128)S(1)} %add_add_fusion.12), channel_id=1, source_target_pairs={{0,8},{8,0},{16,24},{24,16},{1,9},{9,1},{17,25},{25,17},{2,10},{10... | collective-permute-start | bytes 6152 | tf_op jit(solution)/shard_map/ppermute | solution.py:96
  110.9 18.7 %collective-permute-start.14 = (f32[2,256]{1,0:T(2,128)S(1)}, f32[2,256]{1,0:T(2,128)S(1)}, u32[]{:S(2)}, u32[]{:S(2)}) collective-permute-start(f32[2,256]{1,0:T(2,128)S(1)} %add_add_fusion.12), channel_id=1, source_target_pairs={{0,16},{8,24},{16,0},{24,8},{1,17},{9,25},{17,1},{25,9},{2,18},{10... | collective-permute-start | bytes 6152 | tf_op jit(solution)/shard_map/ppermute | solution.py:96
  111.5 18.2 %collective-permute-start.15 = (f32[2,256]{1,0:T(2,128)S(1)}, f32[2,256]{1,0:T(2,128)S(1)}, u32[]{:S(2)}, u32[]{:S(2)}) collective-permute-start(f32[2,256]{1,0:T(2,128)S(1)} %add_add_fusion.12), channel_id=1, source_target_pairs={{0,24},{8,16},{16,8},{24,0},{1,25},{9,17},{17,9},{25,1},{2,26},{10... | collective-permute-start | bytes 6152 | tf_op jit(solution)/shard_map/ppermute | solution.py:96
  133.6 4.5 collective-permute-start.17
  135.2 4.5 collective-permute-start.18
  137.6 5.4 collective-permute-start.19
  143.1 6.1 collective-permute-start.20
  143.7 5.5 collective-permute-start.21
  144.3 4.9 collective-permute-start.22
  161.3 35.1 %collective-permute-start.24 = (bf16[784,1024]{1,0:T(8,128)(2,1)}, bf16[784,1024]{1,0:T(8,128)(2,1)}, u32[]{:S(2)}, u32[]{:S(2)}) collective-permute-start(bf16[784,1024]{1,0:T(8,128)(2,1)} %slice.595), channel_id=1, source_target_pairs={{0,2},{1,3},{2,0},{3,1},{4,6},{5,7},{6,4},{7,5},{8,10},{9,11},{10,... | collective-permute-start | bytes 4816904 | tf_op jit(solution)/shard_map/ppermute | solution.py:96
  161.3 44.4 %collective-permute-start.23 = (bf16[784,1024]{1,0:T(8,128)(2,1)}, bf16[784,1024]{1,0:T(8,128)(2,1)}, u32[]{:S(2)}, u32[]{:S(2)}) collective-permute-start(bf16[784,1024]{1,0:T(8,128)(2,1)} %slice.595), channel_id=1, source_target_pairs={{0,1},{1,0},{2,3},{3,2},{4,5},{5,4},{6,7},{7,6},{8,9},{9,8},{10,11... | collective-permute-start | bytes 4816904 | tf_op jit(solution)/shard_map/ppermute | solution.py:96
  196.5 9.3 %collective-permute-start.25 = (bf16[784,1024]{1,0:T(8,128)(2,1)}, bf16[784,1024]{1,0:T(8,128)(2,1)}, u32[]{:S(2)}, u32[]{:S(2)}) collective-permute-start(bf16[784,1024]{1,0:T(8,128)(2,1)} %collective-permute-done.24), channel_id=1, source_target_pairs={{0,1},{1,0},{2,3},{3,2},{4,5},{5,4},{6,7},{7,6},{8,9},{9,8},{10,11... | collective-permute-start | bytes 4816904 | tf_op jit(solution)/shard_map/ppermute | solution.py:96
  197.2 463.0 %all-reduce.6.cloned.1.call-start = ((), (), s32[]{:S(2)}) async-start(), calls=%async_computation.4 | async-start | bytes 4194304 | tf_op jit(solution)/shard_map/psum | solution.py:365
  205.7 43.4 %collective-permute-start.26 = (bf16[784,512]{1,0:T(8,128)(2,1)S(1)}, bf16[784,512]{1,0:T(8,128)(2,1)S(1)}, u32[]{:S(2)}, u32[]{:S(2)}) collective-permute-start(bf16[784,512]{1,0:T(8,128)(2,1)S(1)} %slice.594), channel_id=1, source_target_pairs={{0,4},{1,5},{2,6},{3,7},{4,0},{5,1},{6,2},{7,3},{8,12},{9,13},{10,... | collective-permute-start | bytes 2408456 | tf_op jit(solution)/shard_map/ppermute | solution.py:96
  261.1 21.4 %collective-permute-start.27 = (f32[784,1]{0,1:T(1,128)S(1)}, f32[784,1]{0,1:T(1,128)S(1)}, u32[]{:S(2)}, u32[]{:S(2)}) collective-permute-start(f32[784,1]{0,1:T(1,128)S(1)} %add.609), channel_id=1, source_target_pairs={{0,4},{1,5},{2,6},{3,7},{4,0},{5,1},{6,2},{7,3},{8,12},{9,13},{10,... | collective-permute-start | bytes 9416 | tf_op jit(solution)/shard_map/ppermute | solution.py:96
  261.2 38.1 %collective-permute-start.28 = (bf16[784,512]{1,0:T(8,128)(2,1)S(1)}, bf16[784,512]{1,0:T(8,128)(2,1)S(1)}, u32[]{:S(2)}, u32[]{:S(2)}) collective-permute-start(bf16[784,512]{1,0:T(8,128)(2,1)S(1)} %fusion.35), channel_id=1, source_target_pairs={{0,4},{1,5},{2,6},{3,7},{4,0},{5,1},{6,2},{7,3},{8,12},{9,13},{10,... | collective-permute-start | bytes 2408456 | tf_op jit(solution)/shard_map/ppermute | solution.py:96
  309.3 4.5 collective-permute-start.30
  309.4 4.7 collective-permute-start.31
  310.7 5.5 collective-permute-start.32
  316.3 3.8 collective-permute-start.33
  317.6 3.7 collective-permute-start.34
  319.1 4.6 collective-permute-start.35
  328.6 35.1 %collective-permute-start.37 = (bf16[784,512]{1,0:T(8,128)(2,1)S(1)}, bf16[784,512]{1,0:T(8,128)(2,1)S(1)}, u32[]{:S(2)}, u32[]{:S(2)}) collective-permute-start(bf16[784,512]{1,0:T(8,128)(2,1)S(1)} %get-tuple-element.329), channel_id=1, source_target_pairs={{0,4},{1,5},{2,6},{3,7},{4,0},{5,1},{6,2},{7,3},{8,12},{9,13},{10,... | collective-permute-start | bytes 2408456 | tf_op jit(solution)/shard_map/ppermute | solution.py:96
  343.0 20.7 %collective-permute-start.36 = (f32[784,2]{0,1:T(2,128)S(1)}, f32[784,2]{0,1:T(2,128)S(1)}, u32[]{:S(2)}, u32[]{:S(2)}) collective-permute-start(f32[784,2]{0,1:T(2,128)S(1)} %pad_maximum_fusion.13), channel_id=1, source_target_pairs={{0,4},{1,5},{2,6},{3,7},{4,0},{5,1},{6,2},{7,3},{8,12},{9,13},{10,... | collective-permute-start | bytes 18824 | tf_op jit(solution)/shard_map/ppermute | solution.py:96
  399.0 5.8 collective-permute-start.39
  411.6 54.5 %collective-permute-start.40 = (bf16[784,1024]{1,0:T(8,128)(2,1)S(1)}, bf16[784,1024]{1,0:T(8,128)(2,1)}, u32[]{:S(2)}, u32[]{:S(2)}) collective-permute-start(bf16[784,1024]{1,0:T(8,128)(2,1)S(1)} %fusion.16), channel_id=1, source_target_pairs={{0,2},{1,3},{2,0},{3,1},{4,6},{5,7},{6,4},{7,5},{8,10},{9,11},{10,... | collective-permute-start | bytes 4816904 | tf_op jit(solution)/shard_map/ppermute | solution.py:96
  417.9 45.9 %collective-permute-start.38 = (bf16[784,512]{1,0:T(8,128)(2,1)S(1)}, bf16[784,512]{1,0:T(8,128)(2,1)S(1)}, u32[]{:S(2)}, u32[]{:S(2)}) collective-permute-start(bf16[784,512]{1,0:T(8,128)(2,1)S(1)} %multiply_convert_fusion.5), channel_id=1, source_target_pairs={{0,4},{1,5},{2,6},{3,7},{4,0},{5,1},{6,2},{7,3},{8,12},{9,13},{10,... | collective-permute-start | bytes 2408456 | tf_op jit(solution)/shard_map/ppermute | solution.py:96
  482.3 4.5 collective-permute-start.42
  482.9 4.5 collective-permute-start.43
  484.2 5.4 collective-permute-start.44
  489.7 4.3 collective-permute-start.45
  490.3 3.7 collective-permute-start.46
  491.1 4.5 collective-permute-start.47
  500.0 18.9 %collective-permute-start.49 = (f32[2,256]{1,0:T(2,128)S(1)}, f32[2,256]{1,0:T(2,128)S(1)}, u32[]{:S(2)}, u32[]{:S(2)}) collective-permute-start(f32[2,256]{1,0:T(2,128)S(1)} %fusion.72), channel_id=1, source_target_pairs={{0,2},{1,3},{2,0},{3,1},{4,6},{5,7},{6,4},{7,5},{8,10},{9,11},{10,... | collective-permute-start | bytes 6152 | tf_op jit(solution)/shard_map/ppermute | solution.py:96
  500.2 18.8 %collective-permute-start.50 = (f32[2,256]{1,0:T(2,128)S(1)}, f32[2,256]{1,0:T(2,128)S(1)}, u32[]{:S(2)}, u32[]{:S(2)}) collective-permute-start(f32[2,256]{1,0:T(2,128)S(1)} %fusion.72), channel_id=1, source_target_pairs={{0,4},{1,5},{2,6},{3,7},{4,0},{5,1},{6,2},{7,3},{8,12},{9,13},{10,... | collective-permute-start | bytes 6152 | tf_op jit(solution)/shard_map/ppermute | solution.py:96
  503.1 15.8 %collective-permute-start.51 = (f32[2,256]{1,0:T(2,128)S(1)}, f32[2,256]{1,0:T(2,128)S(1)}, u32[]{:S(2)}, u32[]{:S(2)}) collective-permute-start(f32[2,256]{1,0:T(2,128)S(1)} %fusion.72), channel_id=1, source_target_pairs={{0,6},{1,7},{2,4},{3,5},{4,2},{5,3},{6,0},{7,1},{8,14},{9,15},{10,... | collective-permute-start | bytes 6152 | tf_op jit(solution)/shard_map/ppermute | solution.py:96
  518.9 7.4 collective-permute-start.52
  520.2 6.1 collective-permute-start.53
  521.7 4.6 collective-permute-start.54
  526.3 299.3 %all-reduce.8.cloned.1.call-start = ((), (), s32[]{:S(2)}) async-start(), calls=%async_computation.5 | async-start | bytes 12845056 | tf_op jit(solution)/shard_map/psum | solution.py:363
  568.4 11.8 %collective-permute-start.55 = (f32[2,256]{1,0:T(2,128)S(1)}, f32[2,256]{1,0:T(2,128)S(1)}, u32[]{:S(2)}, u32[]{:S(2)}) collective-permute-start(f32[2,256]{1,0:T(2,128)S(1)} %pad_maximum_fusion.17), channel_id=1, source_target_pairs={{0,1},{1,0},{2,3},{3,2},{4,5},{5,4},{6,7},{7,6},{8,9},{9,8},{10,11... | collective-permute-start | bytes 6152 | tf_op jit(solution)/shard_map/ppermute | solution.py:96
  580.2 6.1 collective-permute-start.56
  580.3 6.0 collective-permute-start.57
  583.4 5.4 collective-permute-start.58
  588.8 6.0 collective-permute-start.59
  590.2 4.7 collective-permute-start.60
  591.6 4.5 collective-permute-start.61
  666.9 4.8 collective-permute-start.62
  (117 other events, 1719.3 us)
Sparse Core Ops, SparseCore 0:
  10.2 29.8 all-gather.4
  42.3 23.7 all-gather.6
  68.2 38.9 all-gather.8
  197.3 38.8 all-gather.10
  526.4 133.6 all-reduce.5
  667.9 157.5 all-reduce.7
